TPU v7x, 32 devices: a whole 2x2x4 slice. The times are simulated.
32 devices in a mesh: dp: 8 (over z, y), expert: 4 (over x, core).
Axes of the slice: x: 2, y: 2, z: 4, core: 2. Of those that a mesh axis runs over, the one named last changes fastest.
Arguments:
- tokens: bfloat16 [2, 16704, 768], P(None, ('dp', 'expert')), may hold values from -6 to 6
- cotangent: bfloat16 [2, 16704, 768], P(None, ('dp', 'expert')), may hold values from -6 to 6
- item_group: int32 [2, 16704], P(None, ('dp', 'expert')), may hold values from 0 to 1, as said below
- routes: int32 [2, 16704], P(None, ('dp', 'expert')), may hold values from 0 to 2, as said below
- slot_order: int32 [2, 32, 522], P(None, ('dp', 'expert')), may hold values from 0 to 521, each once within a row
- attn_gain: float32 [768], replicated, may hold values from 0.1 to 1.9
- ffn_gain: float32 [768], replicated, may hold values from 0.1 to 1.9
- qkv_weight: bfloat16 [768, 2304], replicated, may hold values from -0.21875 to 0.21875
- out_weight: bfloat16 [768, 768], replicated, may hold values from -0.875 to 0.875
- expert_in: bfloat16 [3, 768, 3072], P(None, None, 'dp'), may hold values from -0.21875 to 0.21875
- expert_out: bfloat16 [3, 3072, 768], P(None, 'dp'), may hold values from -0.109375 to 0.109375
Outputs:
- result: bfloat16 [2, 16704, 768], P(None, ('dp', 'expert'))
- token_grad: bfloat16 [2, 16704, 768], P(None, ('dp', 'expert'))
- attn_gain_grad: float32 [768], replicated
- ffn_gain_grad: float32 [768], replicated
- qkv_grad: float32 [768, 2304], replicated
- out_grad: float32 [768, 768], replicated
- expert_in_grad: float32 [3, 768, 3072], P(None, None, 'dp')
- expert_out_grad: float32 [3, 3072, 768], P(None, 'dp')
Inputs may be any that keep to these rules, and one draw needn't show every extreme that they name: `item_group`: within one device's 522 rows of a micro-batch the first 394 rows are 2 images of 197 tokens numbered 0 to 1 in order, and the rest are 2 captions of 64 tokens, each caption numbered as a different image. `routes`: 0 is the vision expert, 1 the language expert, 2 the vision-language expert. All tokens of one item (an image and its caption) take 2, or none of them does; otherwise image tokens take 0 and caption tokens 1. `slot_order`: each device's 522 entries of a micro-batch are a permutation of 0 to 521.
All inputs are finite; a program needn't handle non-finite values.
Results may differ from a plain program's by a relative error of at most 0.013.
Values may be sent and summed in bfloat16 or wider, within the bound.
A program may use at most 384 MiB of HBM per device.

v0:
```python
import jax
import jax.numpy as jnp
from jax import lax
from jax.sharding import PartitionSpec as P

HEADS = 12


EPSILON = 1e-05


def normalize_parts(v):
    centred = v - jnp.mean(v, axis=-1, keepdims=True)
    inverse = lax.rsqrt(jnp.mean(centred * centred, axis=-1, keepdims=True) + EPSILON)
    return (centred * inverse, inverse)


def normalize_back(grad_unit, unit_rows, inverse):
    return inverse * (
        grad_unit
        - jnp.mean(grad_unit, axis=-1, keepdims=True)
        - unit_rows * jnp.mean(grad_unit * unit_rows, axis=-1, keepdims=True)
    )


def gelu_exact(v):
    return jax.nn.gelu(v, approximate=False)


def contract_rows(former, latter):
    return lax.dot_general(
        former, latter, (((0,), (0,)), ((), ())), preferred_element_type=jnp.float32
    )


def contract_cols(former, latter):
    return lax.dot_general(
        former, latter, (((1,), (1,)), ((), ())), preferred_element_type=jnp.float32
    )


def slot_table(routing, priority, groups_count, capacity):
    length = routing.shape[0]
    position = jnp.zeros((length,), jnp.int32).at[priority].set(jnp.arange(length, dtype=jnp.int32))
    chosen = (routing[priority][:, None] == jnp.arange(3, dtype=jnp.int32)[None, :]).astype(
        jnp.int32
    )
    earlier = jnp.sum((jnp.cumsum(chosen, axis=0) - chosen) * chosen, axis=1)[position]
    replicas = (groups_count - routing + 2) // 3
    target = routing + 3 * (earlier % replicas)
    placing = earlier // replicas
    column = jnp.where(placing < capacity, target * capacity + placing, -1)
    return (
        column[:, None] == jnp.arange(groups_count * capacity, dtype=jnp.int32)[None, :]
    ).astype(jnp.bfloat16)


def attention_scores(qkv_rows, grouping):
    length, triple = qkv_rows.shape
    model_width = triple // 3
    head_dim = model_width // HEADS
    queries = qkv_rows[:, :model_width].reshape(length, HEADS, head_dim)
    keyset = qkv_rows[:, model_width : 2 * model_width].reshape(length, HEADS, head_dim)
    scaling = head_dim ** (-0.5)
    scores = (
        jnp.einsum("qhd,khd->hqk", queries, keyset, preferred_element_type=jnp.float32) * scaling
    )
    within = (grouping[:, None] == grouping[None, :])[None]
    return (jnp.where(within, scores, -1e30), queries, keyset, scaling)


def shards(
    tokens,
    cotangent,
    item_group,
    routes,
    slot_order,
    attn_gain,
    ffn_gain,
    qkv_weight,
    out_weight,
    expert_in,
    expert_out,
):
    groups_count = lax.axis_size("expert")
    hosted = lax.axis_index("expert") % 3
    batches, length, model_width = tokens.shape
    capacity = 2 * length // groups_count
    padded = groups_count * capacity
    head_dim = model_width // HEADS
    in_local = lax.dynamic_index_in_dim(expert_in, hosted, 0, keepdims=False)
    out_local = lax.dynamic_index_in_dim(expert_out, hosted, 0, keepdims=False)
    full_in, full_out = (
        lax.all_gather(in_local, "dp", axis=1, tiled=True),
        lax.all_gather(out_local, "dp", axis=0, tiled=True),
    )
    records = []
    results = []
    for micro_step in range(batches):
        x = tokens[micro_step].astype(jnp.float32)
        unit_one, inverse_one = normalize_parts(x)
        a = (unit_one * attn_gain).astype(jnp.bfloat16)
        qkv_rows = jnp.dot(a, qkv_weight, preferred_element_type=jnp.float32).astype(jnp.bfloat16)
        scores, queries, keyset, scaling = attention_scores(qkv_rows, item_group[micro_step])
        highest = jnp.max(scores, axis=-1, keepdims=True)
        expons = jnp.exp(scores - highest)
        summed = jnp.sum(expons, axis=-1, keepdims=True)
        log_total = highest + jnp.log(summed)
        weights = (expons / summed).astype(jnp.bfloat16)
        valueset = qkv_rows[:, 2 * model_width :].reshape(length, HEADS, head_dim)
        attended = jnp.einsum("hqk,khd->qhd", weights, valueset, preferred_element_type=jnp.float32)
        attended = attended.reshape(length, model_width).astype(jnp.bfloat16)
        y = x + jnp.dot(attended, out_weight, preferred_element_type=jnp.float32)
        unit_two, inverse_two = normalize_parts(y)
        b = (unit_two * ffn_gain).astype(jnp.bfloat16)
        dispatch_table = slot_table(
            routes[micro_step], slot_order[micro_step, 0], groups_count, capacity
        )
        outgoing = (
            contract_rows(dispatch_table, b)
            .astype(jnp.bfloat16)
            .reshape(groups_count, capacity, model_width)
        )
        arrived = lax.all_to_all(
            outgoing, "expert", split_axis=0, concat_axis=0, tiled=True
        ).reshape(padded, model_width)
        hidden = jnp.dot(arrived, full_in, preferred_element_type=jnp.float32)
        expert_rows = jnp.dot(
            gelu_exact(hidden).astype(jnp.bfloat16), full_out, preferred_element_type=jnp.float32
        )
        expert_rows = expert_rows.astype(jnp.bfloat16).reshape(groups_count, capacity, model_width)
        returned = lax.all_to_all(
            expert_rows, "expert", split_axis=0, concat_axis=0, tiled=True
        ).reshape(padded, model_width)
        results.append(
            (y + jnp.dot(dispatch_table, returned, preferred_element_type=jnp.float32)).astype(
                jnp.bfloat16
            )
        )
        kept = (outgoing, None)
        records.append(
            (
                unit_one,
                inverse_one,
                a,
                qkv_rows,
                log_total,
                attended,
                unit_two,
                inverse_two,
                dispatch_table,
                kept,
            )
        )
    grad_in = jnp.zeros(full_in.shape, jnp.float32)
    grad_out = jnp.zeros(full_out.shape, jnp.float32)
    grad_qkv = jnp.zeros(qkv_weight.shape, jnp.float32)
    grad_proj = jnp.zeros(out_weight.shape, jnp.float32)
    grad_gain_one = jnp.zeros(attn_gain.shape, jnp.float32)
    grad_gain_two = jnp.zeros(ffn_gain.shape, jnp.float32)
    token_grads = []
    for micro_step in range(batches):
        (
            unit_one,
            inverse_one,
            a,
            qkv_rows,
            log_total,
            attended,
            unit_two,
            inverse_two,
            dispatch_table,
            kept,
        ) = records[micro_step]
        upstream = cotangent[micro_step]
        grad_sent = (
            contract_rows(dispatch_table, upstream)
            .astype(jnp.bfloat16)
            .reshape(groups_count, capacity, model_width)
        )
        grad_rows = lax.all_to_all(
            grad_sent, "expert", split_axis=0, concat_axis=0, tiled=True
        ).reshape(padded, model_width)
        arrived = lax.all_to_all(
            kept[0], "expert", split_axis=0, concat_axis=0, tiled=True
        ).reshape(padded, model_width)
        hidden = jnp.dot(arrived, full_in, preferred_element_type=jnp.float32)
        activated, gelu_pull = jax.vjp(gelu_exact, hidden)
        grad_out = grad_out + contract_rows(activated.astype(jnp.bfloat16), grad_rows)
        grad_hidden = gelu_pull(contract_cols(grad_rows, full_out))[0].astype(jnp.bfloat16)
        grad_in = grad_in + contract_rows(arrived, grad_hidden)
        grad_back = (
            contract_cols(grad_hidden, full_in)
            .astype(jnp.bfloat16)
            .reshape(groups_count, capacity, model_width)
        )
        grad_returned = lax.all_to_all(
            grad_back, "expert", split_axis=0, concat_axis=0, tiled=True
        ).reshape(padded, model_width)
        grad_norm_two = jnp.dot(dispatch_table, grad_returned, preferred_element_type=jnp.float32)
        grad_gain_two = grad_gain_two + jnp.sum(grad_norm_two * unit_two, axis=0)
        grad_y = upstream.astype(jnp.float32) + normalize_back(
            grad_norm_two * ffn_gain, unit_two, inverse_two
        )
        grad_attn = grad_y.astype(jnp.bfloat16)
        grad_proj = grad_proj + contract_rows(attended, grad_attn)
        grad_mixed = (
            contract_cols(grad_attn, out_weight)
            .astype(jnp.bfloat16)
            .reshape(length, HEADS, head_dim)
        )
        scores, queries, keyset, scaling = attention_scores(qkv_rows, item_group[micro_step])
        valueset = qkv_rows[:, 2 * model_width :].reshape(length, HEADS, head_dim)
        probability = jnp.exp(scores - log_total)
        grad_values = jnp.einsum(
            "hqk,qhd->khd",
            probability.astype(jnp.bfloat16),
            grad_mixed,
            preferred_element_type=jnp.float32,
        )
        grad_probs = jnp.einsum(
            "qhd,khd->hqk", grad_mixed, valueset, preferred_element_type=jnp.float32
        )
        grad_scores = probability * (
            grad_probs - jnp.sum(probability * grad_probs, axis=-1, keepdims=True)
        )
        grad_scores = grad_scores.astype(jnp.bfloat16)
        grad_queries = (
            jnp.einsum("hqk,khd->qhd", grad_scores, keyset, preferred_element_type=jnp.float32)
            * scaling
        )
        grad_keys = (
            jnp.einsum("hqk,qhd->khd", grad_scores, queries, preferred_element_type=jnp.float32)
            * scaling
        )
        grad_triple = jnp.concatenate(
            [
                grad_queries.reshape(length, model_width),
                grad_keys.reshape(length, model_width),
                grad_values.reshape(length, model_width),
            ],
            axis=1,
        ).astype(jnp.bfloat16)
        grad_qkv = grad_qkv + contract_rows(a, grad_triple)
        grad_norm_one = contract_cols(grad_triple, qkv_weight)
        grad_gain_one = grad_gain_one + jnp.sum(grad_norm_one * unit_one, axis=0)
        token_grads.append(
            (grad_y + normalize_back(grad_norm_one * attn_gain, unit_one, inverse_one)).astype(
                jnp.bfloat16
            )
        )
    owned = (jnp.arange(3, dtype=jnp.int32) == hosted)[:, None, None]
    part_in, part_out = (
        lax.psum_scatter(grad_in, "dp", scatter_dimension=1, tiled=True),
        lax.psum_scatter(grad_out, "dp", scatter_dimension=0, tiled=True),
    )
    sum_in, sum_out = lax.psum(
        (jnp.where(owned, part_in[None], 0.0), jnp.where(owned, part_out[None], 0.0)), "expert"
    )
    shared_qkv, shared_proj, shared_one, shared_two = lax.psum(
        (grad_qkv, grad_proj, grad_gain_one, grad_gain_two), ("dp", "expert")
    )
    return (
        jnp.stack(results),
        jnp.stack(token_grads),
        shared_one,
        shared_two,
        shared_qkv,
        shared_proj,
        sum_in,
        sum_out,
    )


def solution(mesh):
    in_specs = (
        P(None, ("dp", "expert"), None),
        P(None, ("dp", "expert"), None),
        P(None, ("dp", "expert")),
        P(None, ("dp", "expert")),
        P(None, ("dp", "expert"), None),
        P(),
        P(),
        P(),
        P(),
        P(None, None, "dp"),
        P(None, "dp", None),
    )
    out_specs = (
        P(None, ("dp", "expert"), None),
        P(None, ("dp", "expert"), None),
        P(),
        P(),
        P(),
        P(),
        P(None, None, "dp"),
        P(None, "dp", None),
    )
    return jax.shard_map(shards, mesh=mesh, in_specs=in_specs, out_specs=out_specs, check_vma=False)
```

profile of v0, /device:TPU:9, one launch (start us, length us, event | category | flops | bytes accessed | tf_op | source)
XLA Modules:
  0.0 1011.5 jit_solution(5243799395549263663)
XLA Ops:
  85.4 9.8 fusion.160
  95.2 8.0 fusion
  103.3 9.6 fusion.87
  142.8 10.0 fusion.158
  153.4 8.5 fusion.1
  166.5 9.7 fusion.86
  176.2 10.1 all-to-all-done.6
  202.1 9.2 all-to-all-done
  227.6 8.8 all-to-all-done.2
  239.4 37.3 %multiply_convert_fusion.2 = (bf16[1044,3072]{1,0:T(8,128)(2,1)}, f32[1044,3072]{1,0:T(8,128)}, f32[1044,3072]{1,0:T(8,128)}) fusion(bf16[1044,768]{1,0:T(8,128)(2,1)} %reshape.477, bf16[1,768,3072]{2,1,0:T(8,128)(2,1)} %all-gather.5.cloned.1.call-done), kind=kOutput, calls=%fused_computation.26 | convolution fusion | flops 5134675968 | bytes 38393856 | tf_op jit(solution)/shard_map/dot_general | solution.py:127
  276.7 33.4 %multiply_convert_fusion.3 = (bf16[1044,3072]{1,0:T(8,128)(2,1)S(1)}, f32[1044,3072]{1,0:T(8,128)}, f32[1044,3072]{1,0:T(8,128)}) fusion(bf16[1044,768]{1,0:T(8,128)(2,1)S(1)} %copy-done.39, bf16[1,768,3072]{2,1,0:T(8,128)(2,1)S(1)} %copy-done.91), kind=kOutput, calls=%fused_computation.39 | convolution fusion | flops 5134675968 | bytes 38393856 | tf_op jit(solution)/shard_map/dot_general | solution.py:127
  317.2 9.3 convolution_add_fusion.1
  326.6 18.1 %add_convert_fusion.1 = bf16[1044,3072]{1,0:T(8,128)(2,1)} fusion(f32[1044,3072]{1,0:T(8,128)} %get-tuple-element.49, bf16[1044,768]{1,0:T(8,128)(2,1)} %reshape.481, f32[1044,3072]{1,0:T(8,128)} %get-tuple-element.77, bf16[1,3072,768]{2,1,0:T(8,128)(2,1)} %all-gather.7.cloned.1.call-done), kind=kOutput, calls=%fused_computation.25 | convolution fusion | flops 4971110400 | bytes 38393856 | tf_op jit(solution)/shard_map/dot_general | solution.py:37
  344.7 11.6 %fusion.162 = f32[768,3072]{1,0:T(8,128)} fusion(bf16[1044,768]{1,0:T(8,128)(2,1)S(1)} %copy-done.40, bf16[1044,3072]{1,0:T(8,128)(2,1)} %add_convert_fusion.1), kind=kOutput, calls=%fused_computation.295 | convolution fusion | flops 4926210048 | bytes 17455104 | tf_op jit(solution)/shard_map/dot_general | solution.py:31
  356.3 18.0 %add_convert_fusion = bf16[1044,3072]{1,0:T(8,128)(2,1)} fusion(f32[1044,3072]{1,0:T(8,128)} %get-tuple-element.53, bf16[1044,768]{1,0:T(8,128)(2,1)} %reshape.489, f32[1044,3072]{1,0:T(8,128)} %get-tuple-element.72, bf16[1,3072,768]{2,1,0:T(8,128)(2,1)} %all-gather.7.cloned.1.call-done), kind=kOutput, calls=%fused_computation.24 | convolution fusion | flops 4971110400 | bytes 38393856 | tf_op jit(solution)/shard_map/dot_general | solution.py:37
  374.3 13.5 %convolution_add_fusion.2 = f32[768,3072]{1,0:T(8,128)} fusion(f32[768,3072]{1,0:T(8,128)} %fusion.162, bf16[1044,768]{1,0:T(8,128)(2,1)S(1)} %copy-done.21, bf16[1044,3072]{1,0:T(8,128)(2,1)} %add_convert_fusion), kind=kOutput, calls=%fused_computation.64 | convolution fusion | flops 4928569344 | bytes 26892288 | tf_op jit(solution)/shard_map/dot_general | solution.py:31
  387.8 9.7 fusion.41
  406.0 9.8 fusion.38
  437.1 13.7 %all-to-all-done.5 = bf16[4,261,768]{2,1,0:T(8,128)(2,1)} async-done(((bf16[4,261,768]{2,1,0:T(8,128)(2,1)}), bf16[4,261,768]{2,1,0:T(8,128)(2,1)}, u32[]{:S(2)}, u32[]{:S(2)}) %all-to-all-start.5) | async-done | bytes 1603616 | tf_op jit(solution)/shard_map/all_to_all | solution.py:197
  479.1 10.7 %multiply_reduce_fusion.1 = (f32[12,522]{1,0:T(8,128)S(1)}, f32[12,522,522]{1,2,0:T(8,128)}) fusion(f32[12,522,522]{1,2,0:T(8,128)} %get-tuple-element.74, f32[12,522]{1,0:T(8,128)S(1)} %copy-done.51, bf16[522,12,64]{0,2,1:T(8,128)(2,1)S(1)} %bitcast.242, bf16[522,12,64]{0,2,1:T(8,128)(2,1)S(1)} %bitcast.247), kind=kOutput, calls=%fused_computation.12 | convolution fusion | flops 428338624 | bytes 27812160 | tf_op jit(solution)/shard_map/qhd,khd->hqk/dot_general | solution.py:221
  489.8 11.8 %multiply_convert_fusion.1 = bf16[12,522,522]{1,2,0:T(8,128)(2,1)S(1)} fusion(f32[12,522,522]{1,2,0:T(8,128)} %get-tuple-element.83, f32[12,522,522]{1,2,0:T(8,128)} %get-tuple-element.74, f32[12,522]{1,0:T(8,128)S(1)} %get-tuple-element.82, f32[12,522]{1,0:T(8,128)S(1)} %copy-done.51), kind=kLoop, calls=%fused_computation.11 | loop fusion | flops 13079232 | bytes 32748192 | tf_op jit(solution)/shard_map/convert_element_type | solution.py:227
  506.1 8.8 fusion.88
  518.4 10.7 %multiply_reduce_fusion = (f32[12,522]{1,0:T(8,128)S(1)}, f32[12,522,522]{1,2,0:T(8,128)}) fusion(f32[12,522,522]{1,2,0:T(8,128)} %get-tuple-element.69, f32[12,522]{1,0:T(8,128)S(1)} %copy-done.50, bf16[522,12,64]{0,2,1:T(8,128)(2,1)S(1)} %bitcast.240, bf16[522,12,64]{0,2,1:T(8,128)(2,1)S(1)} %bitcast.249), kind=kOutput, calls=%fused_computation.9 | convolution fusion | flops 428338624 | bytes 27812160 | tf_op jit(solution)/shard_map/qhd,khd->hqk/dot_general | solution.py:221
  529.1 12.3 %multiply_convert_fusion = bf16[12,522,522]{1,2,0:T(8,128)(2,1)S(1)} fusion(f32[12,522,522]{1,2,0:T(8,128)} %get-tuple-element.81, f32[12,522,522]{1,2,0:T(8,128)} %get-tuple-element.69, f32[12,522]{1,0:T(8,128)S(1)} %get-tuple-element.80, f32[12,522]{1,0:T(8,128)S(1)} %copy-done.50), kind=kLoop, calls=%fused_computation.8 | loop fusion | flops 13079232 | bytes 32748192 | tf_op jit(solution)/shard_map/convert_element_type | solution.py:227
  546.0 8.8 fusion.91
  563.4 9.7 fusion.47
  581.3 9.6 fusion.44
  610.1 16.1 %all-to-all-done.1 = bf16[4,261,768]{2,1,0:T(8,128)(2,1)} async-done(((bf16[4,261,768]{2,1,0:T(8,128)(2,1)}), bf16[4,261,768]{2,1,0:T(8,128)(2,1)}, u32[]{:S(2)}, u32[]{:S(2)}) %all-to-all-start.1) | async-done | bytes 1603616 | tf_op jit(solution)/shard_map/all_to_all | solution.py:132
  636.8 18.3 %reduce-scatter.3.cloned.1.call-done = f32[768,384]{1,0:T(8,128)} async-done(((f32[768,3072]{1,0:T(8,128)}), f32[768,384]{1,0:T(8,128)}) %reduce-scatter.3.cloned.1.call-update) | async-done | bytes 1179664 | tf_op jit(solution)/shard_map/reduce_scatter | solution.py:254
  675.0 42.2 %all-reduce.2 = (f32[768]{0:T(1024)}, f32[768]{0:T(1024)}) all-reduce(f32[768]{0:T(1024)S(1)} %add.246, f32[768]{0:T(1024)S(1)} %add.247), channel_id=1, replica_groups=mesh['dp'=8,'expert'=4] {'dp','expert'}, use_global_device_ids=true, to_apply=%region_32.33 | all-reduce | flops 1536 | bytes 12288 | tf_op jit(solution)/shard_map/psum | solution.py:260
  717.2 137.1 %all-reduce.8.cloned.1.call-done = (f32[768,2304]{1,0:T(8,128)}, f32[768,768]{1,0:T(8,128)}) async-done(((f32[768,2304]{1,0:T(8,128)}, f32[768,768]{1,0:T(8,128)}), (f32[768,2304]{1,0:T(8,128)}, f32[768,768]{1,0:T(8,128)})) %all-reduce.8.cloned.1.call-update) | async-done | bytes 9437200 | tf_op jit(solution)/shard_map/psum | solution.py:260
  854.3 135.4 %all-reduce.10.cloned.1.call-done = (f32[3,768,384]{2,1,0:T(8,128)}, f32[3,384,768]{2,1,0:T(8,128)}) async-done(((f32[3,768,384]{2,1,0:T(8,128)}, f32[3,384,768]{2,1,0:T(8,128)}), (f32[3,768,384]{2,1,0:T(8,128)}, f32[3,384,768]{2,1,0:T(8,128)})) %all-reduce.10.cloned.1.call-update) | async-done | bytes 7077904 | tf_op jit(solution)/shard_map/psum | solution.py:257
  (347 shorter events, 305.9 us)
Async XLA Ops:
  7.2 62.7 %copy-start = (bf16[768,2304]{1,0:T(8,128)(2,1)S(1)}, bf16[768,2304]{1,0:T(8,128)(2,1)}, u32[]{:S(2)}) copy-start(bf16[768,2304]{1,0:T(8,128)(2,1)} %param.18) | copy-start | bytes 10616836
  7.2 232.2 %all-gather.5.cloned.1.call-start = ((), (), s32[]{:S(2)}) async-start(), calls=%async_computation.12 | async-start | bytes 5308416 | tf_op jit(solution)/shard_map/all_gather | solution.py:94
  40.2 14.4 %copy-start.79 = (s32[1024]{0:T(1024)S(1)}, s32[1024]{0:T(1024)}, u32[]{:S(2)}) copy-start(s32[1024]{0:T(1024)} %get-tuple-element.87) | copy-start | bytes 12292
  43.2 118.7 %all-to-all-start.4 = ((bf16[4,261,768]{2,1,0:T(8,128)(2,1)}), bf16[4,261,768]{2,1,0:T(8,128)(2,1)}, u32[]{:S(2)}, u32[]{:S(2)}) async-start(bf16[4,261,768]{2,1,0:T(8,128)(2,1)} %reshape.480), calls=%async_computation.4 | async-start | bytes 3244032 | tf_op jit(solution)/shard_map/all_to_all | solution.py:181
  124.8 69.9 %copy-start.85 = (s32[522]{0:T(1024)}, s32[522]{0:T(1024)S(1)}, u32[]{:S(2)}) copy-start(s32[522]{0:T(1024)S(1)} %fusion.133) | copy-start | bytes 6268
  161.9 24.4 %all-to-all-start.6 = ((bf16[4,261,768]{2,1,0:T(8,128)(2,1)}), bf16[4,261,768]{2,1,0:T(8,128)(2,1)}, u32[]{:S(2)}, u32[]{:S(2)}) async-start(bf16[4,261,768]{2,1,0:T(8,128)(2,1)} %reshape.488), calls=%async_computation.6 | async-start | bytes 3244032 | tf_op jit(solution)/shard_map/all_to_all | solution.py:181
  186.3 25.1 %all-to-all-start = ((bf16[4,261,768]{2,1,0:T(8,128)(2,1)}), bf16[4,261,768]{2,1,0:T(8,128)(2,1)}, u32[]{:S(2)}, u32[]{:S(2)}) async-start(bf16[4,261,768]{2,1,0:T(8,128)(2,1)} %reshape.467), calls=%async_computation | async-start | bytes 3244032 | tf_op jit(solution)/shard_map/all_to_all | solution.py:124
  211.3 25.1 %all-to-all-start.2 = ((bf16[4,261,768]{2,1,0:T(8,128)(2,1)}), bf16[4,261,768]{2,1,0:T(8,128)(2,1)}, u32[]{:S(2)}, u32[]{:S(2)}) async-start(bf16[4,261,768]{2,1,0:T(8,128)(2,1)} %reshape.476), calls=%async_computation.2 | async-start | bytes 3244032 | tf_op jit(solution)/shard_map/all_to_all | solution.py:124
  216.6 110.0 %all-gather.7.cloned.1.call-start = ((), (), s32[]{:S(2)}) async-start(), calls=%async_computation.13 | async-start | bytes 5308416 | tf_op jit(solution)/shard_map/all_gather | solution.py:95
  218.5 414.9 %reduce-scatter.5.cloned.1.call-start = ((), (), s32[]{:S(2)}) async-start(), calls=%async_computation.11 | async-start | bytes 10616832 | tf_op jit(solution)/shard_map/reduce_scatter | solution.py:255
  239.4 37.3 %copy-start.39 = (bf16[1044,768]{1,0:T(8,128)(2,1)S(1)}, bf16[1044,768]{1,0:T(8,128)(2,1)}, u32[]{:S(2)}) copy-start(bf16[1044,768]{1,0:T(8,128)(2,1)} %reshape.468) | copy-start | bytes 4810756
  239.4 37.3 %copy-start.91 = (bf16[1,768,3072]{2,1,0:T(8,128)(2,1)S(1)}, bf16[1,768,3072]{2,1,0:T(8,128)(2,1)}, u32[]{:S(2)}) copy-start(bf16[1,768,3072]{2,1,0:T(8,128)(2,1)} %all-gather.5.cloned.1.call-done) | copy-start | bytes 14155780
  276.7 33.4 %copy-start.38 = (bf16[1044,768]{1,0:T(8,128)(2,1)S(1)}, bf16[1044,768]{1,0:T(8,128)(2,1)}, u32[]{:S(2)}) copy-start(bf16[1044,768]{1,0:T(8,128)(2,1)} %reshape.481) | copy-start | bytes 4810756
  326.5 328.6 %reduce-scatter.3.cloned.1.call-start = ((), (), s32[]{:S(2)}) async-start(), calls=%async_computation.10 | async-start | bytes 10616832 | tf_op jit(solution)/shard_map/reduce_scatter | solution.py:254
  326.6 18.1 %copy-start.40 = (bf16[1044,768]{1,0:T(8,128)(2,1)S(1)}, bf16[1044,768]{1,0:T(8,128)(2,1)}, u32[]{:S(2)}) copy-start(bf16[1044,768]{1,0:T(8,128)(2,1)} %reshape.468) | copy-start | bytes 4810756
  356.3 18.0 %copy-start.21 = (bf16[1044,768]{1,0:T(8,128)(2,1)S(1)}, bf16[1044,768]{1,0:T(8,128)(2,1)}, u32[]{:S(2)}) copy-start(bf16[1044,768]{1,0:T(8,128)(2,1)} %reshape.477) | copy-start | bytes 4810756
  400.5 25.3 %all-to-all-start.7 = ((bf16[4,261,768]{2,1,0:T(8,128)(2,1)}), bf16[4,261,768]{2,1,0:T(8,128)(2,1)}, u32[]{:S(2)}, u32[]{:S(2)}) async-start(bf16[4,261,768]{2,1,0:T(8,128)(2,1)} %reshape.490), calls=%async_computation.7 | async-start | bytes 3244032 | tf_op jit(solution)/shard_map/all_to_all | solution.py:197
  425.8 25.0 %all-to-all-start.5 = ((bf16[4,261,768]{2,1,0:T(8,128)(2,1)}), bf16[4,261,768]{2,1,0:T(8,128)(2,1)}, u32[]{:S(2)}, u32[]{:S(2)}) async-start(bf16[4,261,768]{2,1,0:T(8,128)(2,1)} %reshape.482), calls=%async_computation.5 | async-start | bytes 3244032 | tf_op jit(solution)/shard_map/all_to_all | solution.py:197
  431.0 22.9 %copy-start.74 = (f32[522]{0:T(1024)S(1)}, f32[522]{0:T(1024)}, u32[]{:S(2)}) copy-start(f32[522]{0:T(1024)} %copy-done.73) | copy-start | bytes 6268
  431.0 22.9 %copy-start.81 = (f32[768]{0:T(1024)S(1)}, f32[768]{0:T(1024)}, u32[]{:S(2)}) copy-start(f32[768]{0:T(1024)} %param.17) | copy-start | bytes 9220
  431.0 22.9 %copy-start.84 = (s32[522]{0:T(1024)S(1)}, s32[522]{0:T(1024)}, u32[]{:S(2)}) copy-start(s32[522]{0:T(1024)} %copy-done.82) | copy-start | bytes 6268
  431.0 22.9 %copy-start.90 = (f32[522]{0:T(1024)S(1)}, f32[522]{0:T(1024)}, u32[]{:S(2)}) copy-start(f32[522]{0:T(1024)} %copy-done.89) | copy-start | bytes 6268
  431.0 423.3 %all-reduce.8.cloned.1.call-start = ((), (), s32[]{:S(2)}) async-start(), calls=%async_computation.14 | async-start | bytes 18874368 | tf_op jit(solution)/shard_map/psum | solution.py:260
  489.8 11.8 %copy-start.9 = (bf16[522,768]{0,1:T(8,128)(2,1)S(1)}, bf16[522,768]{0,1:T(8,128)(2,1)}, u32[]{:S(2)}) copy-start(bf16[522,768]{0,1:T(8,128)(2,1)} %copy.51) | copy-start | bytes 2405380
  504.4 10.6 %copy-start.45 = (bf16[12,64,522]{2,1,0:T(8,128)(2,1)}, bf16[12,64,522]{2,1,0:T(8,128)(2,1)S(1)}, u32[]{:S(2)}) copy-start(bf16[12,64,522]{2,1,0:T(8,128)(2,1)S(1)} %multiply_convert_fusion.6) | copy-start | bytes 2405380
  529.1 12.3 %copy-start.10 = (bf16[522,768]{0,1:T(8,128)(2,1)S(1)}, bf16[522,768]{0,1:T(8,128)(2,1)}, u32[]{:S(2)}) copy-start(bf16[522,768]{0,1:T(8,128)(2,1)} %copy.56) | copy-start | bytes 2405380
  544.2 10.5 %copy-start.26 = (bf16[12,64,522]{2,1,0:T(8,128)(2,1)}, bf16[12,64,522]{2,1,0:T(8,128)(2,1)S(1)}, u32[]{:S(2)}) copy-start(bf16[12,64,522]{2,1,0:T(8,128)(2,1)S(1)} %multiply_convert_fusion.4) | copy-start | bytes 2405380
  545.9 9.8 copy-start.2
  545.9 9.8 copy-start.53
  576.2 25.0 %all-to-all-start.3 = ((bf16[4,261,768]{2,1,0:T(8,128)(2,1)}), bf16[4,261,768]{2,1,0:T(8,128)(2,1)}, u32[]{:S(2)}, u32[]{:S(2)}) async-start(bf16[4,261,768]{2,1,0:T(8,128)(2,1)} %reshape.478), calls=%async_computation.3 | async-start | bytes 3244032 | tf_op jit(solution)/shard_map/all_to_all | solution.py:132
  601.2 25.0 %all-to-all-start.1 = ((bf16[4,261,768]{2,1,0:T(8,128)(2,1)}), bf16[4,261,768]{2,1,0:T(8,128)(2,1)}, u32[]{:S(2)}, u32[]{:S(2)}) async-start(bf16[4,261,768]{2,1,0:T(8,128)(2,1)} %reshape.469), calls=%async_computation.1 | async-start | bytes 3244032 | tf_op jit(solution)/shard_map/all_to_all | solution.py:132
  606.4 383.3 %all-reduce.10.cloned.1.call-start = ((), (), s32[]{:S(2)}) async-start(), calls=%async_computation.15 | async-start | bytes 14155776 | tf_op jit(solution)/shard_map/psum | solution.py:257
  (77 other events, 324.2 us)
Sparse Core Ops, SparseCore 0:
  10.1 79.9 all-gather.4
  220.1 78.8 all-gather.6
  326.6 162.4 reduce-scatter.4
  492.5 162.5 reduce-scatter.2
  661.5 192.7 all-reduce.7
  857.2 132.4 all-reduce.9
where the time goes:
time: 1020 us; the launch traced here: 1010 us
  waiting for transfers between devices  363 us (36%)
  matrix products  340 us (33%)
  local copies, waits for them, and re-layouts  138 us (14%)
  other arithmetic  71.2 us (7%)
  blocking collectives  42.2 us (4%)
  starting transfers between devices  41.5 us (4%)
  between operations  15.9 us (2%)
    psum x1, waiting for transfers between devices, shards(): lax.psum((grad_qkv, grad_proj, grad_gain_one, grad_gain_two), ('dp', 'exp...  137 us
    psum x1, waiting for transfers between devices, shards(): lax.psum((jnp.where(owned, part_in[None], 0.0), jnp.where(owned, part_out...  135 us
    dot_general x12, matrix products, contract_rows(): lax.dot_general(former, latter, (((0,), (0,)), ((), ())), preferred_eleme...  71.4 us
    dot_general x2, matrix products, shards(): hidden = jnp.dot(arrived, full_in, preferred_element_type=jnp.float32)  70.7 us
    dot_general x8, matrix products, contract_cols(): lax.dot_general(former, latter, (((1,), (1,)), ((), ())), preferred_eleme...  66.5 us
    psum x1, blocking collectives, shards(): lax.psum((grad_qkv, grad_proj, grad_gain_one, grad_gain_two), ('dp', 'exp...  42.2 us
    unnamed x198, local copies, waits for them, and re-layouts  27.5 us
    convert_element_type x2, other arithmetic, shards(): grad_scores = grad_scores.astype(jnp.bfloat16)  24.1 us
  transfers between devices with their start and end apart: 14, of which 10 were waited for; matrix products, arithmetic and copies ran while one was open for 52% of the time, Pallas kernels for 0%

commit v1 on v0

v1 whole, which is shorter than its diff:
```python
import functools

import jax
import jax.numpy as jnp
from jax import lax
from jax.experimental import pallas as pl
from jax.experimental.pallas import tpu as pltpu
from jax.sharding import PartitionSpec as P

HEADS = 12
EPSILON = 1e-05
PATCHES = 197
CAPTION = 64
ITEMS = 2
IMAGE_ROWS = 208
ITEM_ROWS = IMAGE_ROWS + CAPTION
ROWS = ITEMS * ITEM_ROWS
FLAG_ROWS = 16
TILE = 256
VMEM_LIMIT = 60 * 1024 * 1024
F32 = jnp.float32
BF16 = jnp.bfloat16


def dot(a, b, a_dim, b_dim):
    return lax.dot_general(
        a, b, (((a_dim,), (b_dim,)), ((), ())), preferred_element_type=F32
    )


def normalize_parts(v):
    centred = v - jnp.mean(v, axis=-1, keepdims=True)
    inverse = lax.rsqrt(jnp.mean(centred * centred, axis=-1, keepdims=True) + EPSILON)
    return centred * inverse, inverse


def normalize_back(grad_unit, unit_rows, inverse):
    return inverse * (
        grad_unit
        - jnp.mean(grad_unit, axis=-1, keepdims=True)
        - unit_rows * jnp.mean(grad_unit * unit_rows, axis=-1, keepdims=True)
    )


def gelu_and_slope(h):
    bell = jnp.exp(-0.5 * h * h)
    t = 1.0 / (1.0 + (0.3275911 * 0.7071067811865476) * jnp.abs(h))
    poly = t * (
        0.254829592
        + t * (-0.284496736 + t * (1.421413741 + t * (-1.453152027 + t * 1.061405429)))
    )
    below = 0.5 * poly * bell
    phi = jnp.where(h > 0, 1.0 - below, below)
    return h * phi, phi + h * (0.3989422804014327 * bell)


class Partners:
    def __init__(self):
        dp, expert = lax.axis_index("dp"), lax.axis_index("expert")
        self.core = (dp, expert + 1 - 2 * (expert % 2))
        self.x = (dp, (expert + 2) % 4)
        self.y = (dp + 1 - 2 * (dp % 2), expert)
        self.z = {shift: ((dp + 2 * shift) % 8, expert) for shift in (1, 2, 3)}
        self.z_pair = (dp + 2 - 4 * (dp // 2 % 2), expert)

    def greet(self):
        barrier = pltpu.get_barrier_semaphore()
        everyone = [self.core, self.x, self.y, self.z[1], self.z[2], self.z[3]]
        for other in everyone:
            pl.semaphore_signal(
                barrier, inc=1, device_id=other, device_id_type=pl.DeviceIdType.MESH
            )
        pl.semaphore_wait(barrier, len(everyone))


class Copies:
    def __init__(self, send_sem, recv_sem, local_sem):
        self.send_sem, self.recv_sem, self.local_sem = send_sem, recv_sem, local_sem
        self.sent, self.kept, self.locals = [], [], 0

    def send(self, src, dst, device):
        at = len(self.sent)
        copy = pltpu.make_async_remote_copy(
            src_ref=src,
            dst_ref=dst,
            send_sem=self.send_sem.at[at],
            recv_sem=self.recv_sem.at[at],
            device_id=device,
            device_id_type=pl.DeviceIdType.MESH,
        )
        copy.start()
        self.sent.append(copy)
        return copy

    def keep(self, src, dst):
        copy = self.load(src, dst)
        self.kept.append(copy)
        return copy

    def load(self, src, dst):
        copy = pltpu.make_async_copy(src, dst, self.local_sem.at[self.locals])
        self.locals += 1
        copy.start()
        return copy

    def finish(self):
        for copy in self.sent:
            copy.wait_send()
        for copy in self.kept:
            copy.wait()


def pick_rows(index_ref, m, length, rows=slice(0, ROWS)):
    token = lax.broadcasted_iota(jnp.int32, (rows.stop - rows.start, length), 1)
    return index_ref[m, rows] == token


def front_kernel(direct, batches, *refs):
    (own_ref, tokens_ref, cot_ref, index_ref, keep_ref, flags_ref, gain1_ref, gain2_ref) = refs[:8]
    wqkv_ref, wo_ref, w_all, gz_all, flags_all, b_all, x_out, qkv_out, p_out, o_out, y_out = refs[
        8:19
    ]
    gz_scr, b_scr, x_scr, qkv_scr, p_scr, o_scr, y_scr, send_sem, recv_sem, local_sem = refs[19:]
    length, width = tokens_ref.shape[1:]
    head_dim = width // HEADS
    pair = 2 * head_dim
    copies = Copies(send_sem, recv_sem, local_sem)

    def spread(src, slots):
        copies.keep(src, slots(0))
        if not direct:
            return None
        near = copies.send(src, slots(1), near_by.core)
        return near, copies.send(src, slots(2), near_by.x)

    def pass_on(pair_of, slots):
        near, far = pair_of
        far.wait_recv()
        return near, copies.send(slots(2), slots(3), near_by.core)

    if direct:
        near_by = Partners()
        near_by.greet()
        y0 = copies.send(own_ref, w_all.at[0], near_by.y)
        z1 = copies.send(own_ref, w_all.at[1], near_by.z[1])
    flags = spread(flags_ref, lambda i: flags_all.at[i])

    for m in range(batches):
        chosen = pick_rows(index_ref, m, length) & (keep_ref[m] > 0)
        gz_scr[m] = dot(chosen.astype(BF16), cot_ref[m], 1, 0).astype(BF16)
    gz = spread(gz_scr, lambda i: gz_all.at[i])

    left = lax.broadcasted_iota(jnp.int32, (ITEM_ROWS, pair), 1) < head_dim
    key = lax.broadcasted_iota(jnp.int32, (1, ITEM_ROWS), 1)
    bias = jnp.where((key >= PATCHES) & (key < IMAGE_ROWS), -1e30, 0.0).astype(F32)
    b_sent = []
    for m in range(batches):
        xb = dot(pick_rows(index_ref, m, length).astype(BF16), tokens_ref[m], 1, 0)
        x_scr[m] = xb.astype(BF16)
        unit, _ = normalize_parts(xb)
        a = (unit * gain1_ref[...]).astype(BF16)
        for part in range(3):
            cols = slice(part * width, (part + 1) * width)
            qkv_scr[m, :, cols] = dot(a, wqkv_ref[:, cols], 1, 0).astype(BF16)

        def heads(hp, carry, m=m):
            at_q = pl.ds(pl.multiple_of(hp * pair, pair), pair)
            at_k = pl.ds(pl.multiple_of(width + hp * pair, pair), pair)
            at_v = pl.ds(pl.multiple_of(2 * width + hp * pair, pair), pair)
            for item in range(ITEMS):
                rows = slice(item * ITEM_ROWS, (item + 1) * ITEM_ROWS)
                q, k, v = qkv_scr[m, rows, at_q], qkv_scr[m, rows, at_k], qkv_scr[m, rows, at_v]
                outs = []
                for half in range(2):
                    mine = left if half == 0 else ~left
                    s = dot(jnp.where(mine, q, 0), k, 1, 1) * (head_dim**-0.5) + bias
                    e = jnp.exp(s - jnp.max(s, axis=-1, keepdims=True))
                    p = (e * (1.0 / jnp.sum(e, axis=-1, keepdims=True))).astype(BF16)
                    p_scr[m, item, hp * 2 + half] = p
                    outs.append(dot(p, v, 1, 0))
                o_scr[m, rows, at_q] = jnp.where(left, outs[0], outs[1]).astype(BF16)
            return carry

        lax.fori_loop(0, HEADS // 2, heads, 0)
        y = x_scr[m].astype(F32) + dot(o_scr[m], wo_ref[...], 1, 0)
        y_scr[m] = y
        unit2, _ = normalize_parts(y)
        b_scr[m] = (unit2 * gain2_ref[...]).astype(BF16)
        b_sent.append(spread(b_scr.at[m], lambda i, m=m: b_all.at[i, m]))
        for scr, out in (
            (x_scr, x_out), (qkv_scr, qkv_out), (p_scr, p_out), (o_scr, o_out), (y_scr, y_out)
        ):
            copies.keep(scr.at[m], out.at[m])
        if direct and m == 0:
            z1.wait_recv()
            y1 = copies.send(w_all.at[1], w_all.at[2], near_by.y)
            z3 = copies.send(own_ref, w_all.at[3], near_by.z[3])
            flags = pass_on(flags, lambda i: flags_all.at[i])

    if direct:
        z3.wait_recv()
        y3 = copies.send(w_all.at[3], w_all.at[4], near_by.y)
        z2 = [copies.send(own_ref.at[:, i], w_all.at[5, :, i], near_by.z[2]) for i in range(2)]
        gz = pass_on(gz, lambda i: gz_all.at[i])
        b_sent[0] = pass_on(b_sent[0], lambda i: b_all.at[i, 0])
        y2 = []
        for i in range(2):
            z2[i].wait_recv()
            y2.append(copies.send(w_all.at[5, :, i], w_all.at[6, :, i], near_by.y))
        for m in range(1, batches):
            b_sent[m] = pass_on(b_sent[m], lambda i, m=m: b_all.at[i, m])
        for copy in [y0, y1, y3, *y2, *flags, *gz] + [c for pair_of in b_sent for c in pair_of]:
            copy.wait_recv()
    copies.finish()


def front(direct, own, tokens, cot, index, keep, flags, gain1, gain2, wqkv, wo):
    batches, length, width = tokens.shape
    groups = 4 if direct else 1
    out = jax.ShapeDtypeStruct
    vmem = pl.BlockSpec(memory_space=pltpu.VMEM)
    anywhere = pl.BlockSpec(memory_space=pl.ANY)
    kept = [
        ((batches, ROWS, width), BF16),
        ((batches, ROWS, 3 * width), BF16),
        ((batches, ITEMS, HEADS, ITEM_ROWS, ITEM_ROWS), BF16),
        ((batches, ROWS, width), BF16),
        ((batches, ROWS, width), F32),
    ]
    scratch = [pltpu.VMEM((batches, ROWS, width), BF16)] * 2
    return pl.pallas_call(
        functools.partial(front_kernel, direct, batches),
        in_specs=[anywhere] + [vmem] * 9,
        out_specs=[anywhere] * 9,
        out_shape=[
            out((7 if direct else 1,) + (own.shape if direct else (8, 128)), BF16),
            out((groups, batches, ROWS, width), BF16),
            out((groups,) + flags.shape, flags.dtype),
            out((groups, batches, ROWS, width), BF16),
        ]
        + [out(*k) for k in kept],
        scratch_shapes=scratch
        + [pltpu.VMEM(*k) for k in kept]
        + [
            pltpu.SemaphoreType.DMA((32,)),
            pltpu.SemaphoreType.DMA((32,)),
            pltpu.SemaphoreType.DMA((24,)),
        ],
        compiler_params=pltpu.CompilerParams(
            vmem_limit_bytes=VMEM_LIMIT,
            has_side_effects=direct,
            collective_id=0 if direct else None,
        ),
        cost_estimate=pl.CostEstimate(
            flops=batches
            * (2 * ROWS * width * width * 4 + 8 * HEADS * ITEMS * ITEM_ROWS**2 * 128),
            bytes_accessed=60_000_000,
            transcendentals=batches * HEADS * ITEMS * ITEM_ROWS**2,
        ),
        name="front",
    )(own, tokens, cot, index, keep, flags, gain1, gain2, wqkv, wo)


def head_gradients(qkv_at, go_at, p_of, gqkv_ref, row0, hp, width, left):
    head_dim = width // HEADS
    pair = 2 * head_dim
    scaling = head_dim**-0.5
    at_q = pl.ds(pl.multiple_of(hp * pair, pair), pair)
    at_k = pl.ds(pl.multiple_of(width + hp * pair, pair), pair)
    at_v = pl.ds(pl.multiple_of(2 * width + hp * pair, pair), pair)
    for item in range(ITEMS):
        rows = slice(item * ITEM_ROWS, (item + 1) * ITEM_ROWS)
        out_rows = slice(row0 + rows.start, row0 + rows.stop)
        q, k, v = qkv_at(rows, at_q), qkv_at(rows, at_k), qkv_at(rows, at_v)
        go = go_at(rows, at_q)
        gq, gk, gv = [], [], []
        for half in range(2):
            mine = left if half == 0 else ~left
            p = p_of(item, half)
            pf = p.astype(F32)
            gp = dot(jnp.where(mine, go, 0), v, 1, 1)
            gs = (pf * (gp - jnp.sum(pf * gp, axis=-1, keepdims=True))).astype(BF16)
            gv.append(dot(p, go, 0, 0))
            gq.append(dot(gs, k, 1, 0))
            gk.append(dot(gs, q, 0, 0))
        gqkv_ref[out_rows, at_q] = (jnp.where(left, gq[0], gq[1]) * scaling).astype(BF16)
        gqkv_ref[out_rows, at_k] = (jnp.where(left, gk[0], gk[1]) * scaling).astype(BF16)
        gqkv_ref[out_rows, at_v] = jnp.where(left, gv[0], gv[1]).astype(BF16)


def back_kernel(batches, *refs):
    gb_parts, z_parts, gw, cot_in, index_ref, keep_ref, x_in, o_in, y_in, qkv_in, p_in = refs[:11]
    gain1_ref, gain2_ref, wqkv_in, wo_in = refs[11:15]
    result_out, tg_out, gall, wsum, gains_out, z_core, z_far, rs_z = refs[15:23]
    (
        wqkv, wo, x, o, y, cot, qkv, p, gb_own, gb_far, gb_core, gb_cross, gb_x,
        gy, ga, go, gqkv, grads, r_core, r_one, r_two, r_z, final,
        held, r_y, gsum, gain_in, tok, send_sem, recv_sem, local_sem, p_sem,
    ) = refs[23:]
    width = x.shape[1]
    head_dim = width // HEADS
    pair = 2 * head_dim
    length = cot.shape[0]
    dp, expert = lax.axis_index("dp"), lax.axis_index("expert")
    core, xi, yi, zi = expert % 2, expert // 2, dp % 2, dp // 2
    copies = Copies(send_sem, recv_sem, local_sem)
    near_by = Partners()
    near_by.greet()
    load, send = copies.load, copies.send

    def add(*terms):
        total = terms[0].astype(F32)
        for term in terms[1:]:
            total = total + term.astype(F32)
        return total.astype(BF16)

    crossed, nearer = [], []
    for m in range(batches):
        crossed.append(send(gb_parts.at[3, m], gb_cross.at[m], near_by.core))
        nearer.append(send(gb_parts.at[1, m], gb_core.at[m], near_by.core))
    order = ((6, 2), (2, 3), (4, 1), (0, 0))
    pieces = [send(gw.at[order[0][0] + 1], r_y.at[0], near_by.y)]
    far_loads = [load(gb_parts.at[2, m], gb_far.at[m]) for m in range(batches)]
    own_loads = [load(gb_parts.at[0, m], gb_own.at[m]) for m in range(batches)]
    first_loads = [load(y_in.at[0], y), load(cot_in.at[0], cot)]
    held_loads = [load(gw.at[order[i][0]], held.at[i]) for i in range(4)]
    late_loads = [load(o_in, o), load(wo_in, wo), load(qkv_in.at[0], qkv)]
    last_loads = [load(x_in, x), load(wqkv_in, wqkv)]
    along = []
    for m in range(batches):
        far_loads[m].wait()
        crossed[m].wait_recv()
        gb_far[m] = add(gb_far[m], gb_cross[m])
        along.append(send(gb_far.at[m], gb_x.at[m], near_by.x))
    z_crossed = [send(z_parts.at[3, m], z_core.at[1, m], near_by.core) for m in range(batches)]
    z_nearer = [send(z_parts.at[1, m], z_core.at[0, m], near_by.core) for m in range(batches)]

    sent_z = []

    def reduce_piece(i):
        pieces[i].wait_recv()
        if i < 3:
            pieces.append(send(gw.at[order[i + 1][0] + 1], r_y.at[i + 1], near_by.y))
        held_loads[i].wait()
        held[i] = add(held[i], r_y[i])
        if i < 3:
            sent_z.append(send(held.at[i], rs_z.at[i], near_by.z[order[i][1]]))

    left = lax.broadcasted_iota(jnp.int32, (ITEM_ROWS, pair), 1) < head_dim
    reduce_piece(0)
    for copy in first_loads + late_loads:
        copy.wait()
    gain2_grad = jnp.zeros((1, width), F32)
    items = [slice(i * ITEM_ROWS, (i + 1) * ITEM_ROWS) for i in range(ITEMS)]
    for m in range(batches):
        row0 = m * ROWS

        def p_load(hp, m=m):
            return pltpu.make_async_copy(
                p_in.at[m, :, pl.ds(2 * hp, 2)], p.at[hp % 2], p_sem.at[hp % 2]
            )

        p_load(0).start()
        own_loads[m].wait()
        nearer[m].wait_recv()
        along[m].wait_recv()
        for rows in items:
            at = slice(row0 + rows.start, row0 + rows.stop)
            gb = (
                gb_own[m, rows].astype(F32)
                + gb_core[m, rows].astype(F32)
                + gb_x[m, rows].astype(F32)
            )
            unit2, inverse2 = normalize_parts(y[rows])
            gain2_grad = gain2_grad + jnp.sum(gb * unit2, axis=0, keepdims=True)
            g = dot(pick_rows(index_ref, m, length, rows).astype(BF16), cot[...], 1, 0)
            gy_rows = g + normalize_back(gb * gain2_ref[...], unit2, inverse2)
            gy[at] = gy_rows
            ga[at] = gy_rows.astype(BF16)
            go[rows] = dot(ga[at], wo[...], 1, 1).astype(BF16)
        if m + 1 < batches:
            first_loads = [load(y_in.at[m + 1], y), load(cot_in.at[m + 1], cot)]

        def heads(hp, carry, row0=row0, p_load=p_load):
            @pl.when(hp + 1 < HEADS // 2)
            def _():
                p_load(hp + 1).start()

            p_load(hp).wait()
            slot = hp % 2
            head_gradients(
                lambda rows, cols: qkv[rows, cols],
                lambda rows, cols: go[rows, cols],
                lambda item, half: p[slot, item, half],
                gqkv, row0, hp, width, left,
            )
            return carry

        lax.fori_loop(0, HEADS // 2, heads, 0)
        if m + 1 < batches:
            first_loads.append(load(qkv_in.at[m + 1], qkv))
            reduce_piece(1 + m)
            for copy in first_loads:
                copy.wait()

    z_along = []
    for m in range(batches):
        loads = [load(z_parts.at[2, m], gb_own.at[m])]
        z_crossed[m].wait_recv()
        loads.append(load(z_core.at[1, m], gb_core.at[m]))
        for copy in loads:
            copy.wait()
        gb_cross[m] = add(gb_own[m], gb_core[m])
        z_along.append(send(gb_cross.at[m], z_far.at[m], near_by.x))
    reduce_piece(2)

    for copy in last_loads:
        copy.wait()
    for part in range(2):
        cols = slice(part * width // 2, (part + 1) * width // 2)
        grads[:, 3 * width + cols.start : 3 * width + cols.stop] = dot(
            o[...], ga[:, cols], 0, 0
        ).astype(BF16)
    a = ga
    for m in range(batches):
        at = slice(m * ROWS, (m + 1) * ROWS)
        unit, _ = normalize_parts(x[at].astype(F32))
        a[at] = (unit * gain1_ref[...]).astype(BF16)
    for part in range(6):
        cols = slice(part * width // 2, (part + 1) * width // 2)
        grads[:, cols] = dot(a[...], gqkv[:, cols], 0, 0).astype(BF16)

    half = width // 2
    wide = grads.shape[1] // 2
    a_cols, b_cols = pl.ds(0, wide), pl.ds(wide, wide)

    def rows_at(start, size):
        return pl.ds(pl.multiple_of(start, 32), size)

    row_c = core * half
    copy_c = send(grads.at[rows_at(half - row_c, half)], r_core, near_by.core)

    gain1_grad = jnp.zeros((1, width), F32)
    token_stores = []
    for m in range(batches):
        for rows in items:
            at = slice(m * ROWS + rows.start, m * ROWS + rows.stop)
            unit, inverse = normalize_parts(x[at].astype(F32))
            gnorm = dot(gqkv[at], wqkv[...], 1, 1)
            gain1_grad = gain1_grad + jnp.sum(gnorm * unit, axis=0, keepdims=True)
            go[rows] = (gy[at] + normalize_back(gnorm * gain1_ref[...], unit, inverse)).astype(BF16)
        tok[m] = dot(pick_rows(index_ref, m, length).astype(BF16), go[...], 0, 0).astype(BF16)
        token_stores.append(load(tok.at[m], tg_out.at[m]))
        if m == 0:
            copy_c.wait_recv()
            for part in range(8):
                cols = pl.ds(part * width // 2, width // 2)
                grads[rows_at(row_c, half), cols] = add(
                    grads[rows_at(row_c, half), cols], r_core[:, cols]
                )
            quarter = half // 2
            row_a, row_b = row_c + xi * quarter, row_c + yi * quarter
            one = [
                send(
                    grads.at[rows_at(row_c + (1 - xi) * quarter, quarter), a_cols],
                    r_one.at[0], near_by.x,
                ),
                send(
                    grads.at[rows_at(row_c + (1 - yi) * quarter, quarter), b_cols],
                    r_one.at[1], near_by.y,
                ),
            ]
    gsum[0] = jnp.concatenate([gain1_grad, gain2_grad, jnp.zeros((6, width), F32)], axis=0)
    gain_partners = [near_by.core, near_by.x, near_by.y, near_by.z_pair, near_by.z[2]]
    gain_sent = [send(gsum.at[0], gain_in.at[0], gain_partners[0])]

    def gain_step():
        at = len(gain_sent)
        gain_sent[-1].wait_recv()
        gsum[at] = gsum[at - 1] + gain_in[at - 1]
        if at < len(gain_partners):
            gain_sent.append(send(gsum.at[at], gain_in.at[at], gain_partners[at]))

    gain_step()
    reduce_piece(3)
    for i, (row, cols) in enumerate(((row_a, a_cols), (row_b, b_cols))):
        one[i].wait_recv()
        grads[rows_at(row, quarter), cols] = add(grads[rows_at(row, quarter), cols], r_one[i])
    eighth = quarter // 2
    two = [
        send(
            grads.at[rows_at(row_a + (1 - yi) * eighth, eighth), a_cols], r_two.at[0], near_by.y
        ),
        send(
            grads.at[rows_at(row_b + (1 - xi) * eighth, eighth), b_cols], r_two.at[1], near_by.x
        ),
    ]
    row_a2, row_b2 = row_a + yi * eighth, row_b + xi * eighth
    gain_step()

    for m in range(batches):
        z_nearer[m].wait_recv()
        z_along[m].wait_recv()
        loads = [
            load(z_parts.at[0, m], gb_own.at[m]),
            load(z_core.at[0, m], gb_core.at[m]),
            load(z_far.at[m], gb_x.at[m]),
            load(y_in.at[m], y),
        ]
        for copy in loads:
            copy.wait()
        for rows in items:
            chosen = pick_rows(index_ref, m, length, rows)
            keep = jnp.sum(jnp.where(chosen, keep_ref[m], 0.0), axis=1, keepdims=True)
            z = (
                gb_own[m, rows].astype(F32)
                + gb_core[m, rows].astype(F32)
                + gb_x[m, rows].astype(F32)
            )
            go[rows] = (y[rows] + jnp.where(keep > 0, z, 0.0)).astype(BF16)
        token_stores[m].wait()
        tok[m] = dot(pick_rows(index_ref, m, length).astype(BF16), go[...], 0, 0).astype(BF16)
        copies.keep(tok.at[m], result_out.at[m])

    for i, (row, cols) in enumerate(((row_a2, a_cols), (row_b2, b_cols))):
        two[i].wait_recv()
        grads[rows_at(row, eighth), cols] = add(grads[rows_at(row, eighth), cols], r_two[i])
    chunk = wide // 4
    ends = ((row_a2, 0), (row_b2, wide))

    def z_cols(first, z):
        return pl.ds(pl.multiple_of(first + z * chunk, 128), chunk)

    three = [
        [
            send(
                grads.at[rows_at(row, eighth), z_cols(first, (zi + shift) % 4)],
                r_z.at[i, shift - 1], near_by.z[shift],
            )
            for shift in (1, 2, 3)
        ]
        for i, (row, first) in enumerate(ends)
    ]
    gain_step()

    z_loads = []
    for i in range(3):
        sent_z[i].wait_recv()
        z_loads.append(load(rs_z.at[i], r_y.at[i]))
    for copy in z_loads:
        copy.wait()
    held[3] = add(held[3], r_y[0], r_y[1], r_y[2])
    copies.keep(held.at[3], wsum.at[expert])
    join_near = send(held.at[3], wsum.at[expert], near_by.core)
    join_far = send(held.at[3], wsum.at[expert], near_by.x)

    spread = []
    for i, (row, first) in enumerate(ends):
        for copy in three[i]:
            copy.wait_recv()
        mine = z_cols(first, zi)
        final[i] = add(grads[rows_at(row, eighth), mine], r_z[i, 0], r_z[i, 1], r_z[i, 2])
        place = gall.at[rows_at(row, eighth), mine]
        spread.append(
            (
                load(final.at[i], place),
                [send(final.at[i], place, near_by.z[shift]) for shift in (1, 2, 3)],
            )
        )
    gain_step()
    join_far.wait_recv()
    opposite = (expert + 2) % 4
    join_last = send(wsum.at[opposite], wsum.at[opposite], near_by.core)

    def block(row, size, cols):
        return gall.at[rows_at(row, size), cols]

    back_two = []
    for i, (row, cols, to) in enumerate(
        ((row_a2, a_cols, near_by.y), (row_b2, b_cols, near_by.x))
    ):
        own, others = spread[i]
        own.wait()
        for copy in others:
            copy.wait_recv()
        back_two.append(send(block(row, eighth, cols), block(row, eighth, cols), to))
    gain_step()
    copies.keep(gsum.at[len(gain_partners)], gains_out)
    back_one = []
    for i, (row, cols, to) in enumerate(((row_a, a_cols, near_by.x), (row_b, b_cols, near_by.y))):
        back_two[i].wait_recv()
        back_one.append(send(block(row, quarter, cols), block(row, quarter, cols), to))
    back_core = []
    for i, cols in enumerate((a_cols, b_cols)):
        back_one[i].wait_recv()
        back_core.append(send(block(row_c, half, cols), block(row_c, half, cols), near_by.core))
    for copy in [join_near, join_last] + back_core:
        copy.wait_recv()
    copies.finish()


def back(gb_parts, z_parts, gw, cot, index, keep, x, o, y, qkv, p, gain1, gain2, wqkv, wo):
    batches, rows, width = x.shape
    length = cot.shape[1]
    out = jax.ShapeDtypeStruct
    vmem = pl.BlockSpec(memory_space=pltpu.VMEM)
    anywhere = pl.BlockSpec(memory_space=pl.ANY)
    piece = gw.shape[1:]
    both = batches * rows
    half, wide = width // 2, 2 * width
    tokens_shape = (batches, rows, width)
    slots = [tokens_shape] * 5
    scratch = [
        ((width, 3 * width), BF16),
        ((width, width), BF16),
        ((both, width), BF16),
        ((both, width), BF16),
        ((rows, width), F32),
        ((length, width), BF16),
        ((rows, 3 * width), BF16),
        ((2, ITEMS, 2, ITEM_ROWS, ITEM_ROWS), BF16),
        *[(slot, BF16) for slot in slots],
        ((both, width), F32),
        ((both, width), BF16),
        ((rows, width), BF16),
        ((both, 3 * width), BF16),
        ((width, 4 * width), BF16),
        ((half, 4 * width), BF16),
        ((2, half // 2, wide), BF16),
        ((2, half // 4, wide), BF16),
        ((2, 3, half // 4, wide // 4), BF16),
        ((2, half // 4, wide // 4), BF16),
        ((4,) + piece, BF16),
        ((4,) + piece, BF16),
        ((6, 8, width), F32),
        ((5, 8, width), F32),
        ((batches, length, width), BF16),
    ]
    return pl.pallas_call(
        functools.partial(back_kernel, batches),
        in_specs=[anywhere] * 4 + [vmem] * 2 + [anywhere] * 5 + [vmem] * 2 + [anywhere] * 2,
        out_specs=[anywhere] * 8,
        out_shape=[
            out(cot.shape, BF16),
            out(cot.shape, BF16),
            out((width, 4 * width), BF16),
            out((4,) + piece, BF16),
            out((8, width), F32),
            out((2,) + tokens_shape, BF16),
            out(tokens_shape, BF16),
            out((3,) + piece, BF16),
        ],
        scratch_shapes=[pltpu.VMEM(*k) for k in scratch]
        + [
            pltpu.SemaphoreType.DMA((64,)),
            pltpu.SemaphoreType.DMA((64,)),
            pltpu.SemaphoreType.DMA((64,)),
            pltpu.SemaphoreType.DMA((2,)),
        ],
        compiler_params=pltpu.CompilerParams(
            vmem_limit_bytes=VMEM_LIMIT, has_side_effects=True, collective_id=1
        ),
        cost_estimate=pl.CostEstimate(
            flops=batches
            * (2 * rows * width * width * 8 + 16 * HEADS * ITEMS * ITEM_ROWS**2 * 128),
            bytes_accessed=80_000_000,
            transcendentals=0,
        ),
        name="back",
    )(
        gb_parts, z_parts, gw, cot, index, keep,
        x.reshape(both, width), o.reshape(both, width), y, qkv, p, gain1, gain2, wqkv, wo,
    )


def attention_backward_kernel(n_parts, n_carry, *refs):
    parts = refs[:n_parts]
    (cot_ref, x_ref, y_ref, qkv_ref, p_ref, o_ref, gain1_ref, gain2_ref, wqkv_ref, wo_ref) = refs[
        n_parts : n_parts + 10
    ]
    carried = refs[n_parts + 10 : n_parts + 10 + n_carry]
    tg_ref, gwqkv_ref, gwo_ref, ggain_ref, gmix_ref, gqkv_ref = refs[n_parts + 10 + n_carry :]
    width = x_ref.shape[1]
    head_dim = width // HEADS
    gb = parts[0][...].astype(F32)
    for part in parts[1:]:
        gb = gb + part[...].astype(F32)
    unit2, inverse2 = normalize_parts(y_ref[...])
    gain2_grad = jnp.sum(gb * unit2, axis=0, keepdims=True)
    gy = cot_ref[...].astype(F32) + normalize_back(gb * gain2_ref[...], unit2, inverse2)
    ga = gy.astype(BF16)
    gwo = dot(o_ref[...], ga, 0, 0)
    if n_carry:
        gwo = gwo + carried[1][...]
    gwo_ref[...] = gwo
    gmix_ref[...] = dot(ga, wo_ref[...], 1, 1).astype(BF16)
    pair = 2 * head_dim
    left = lax.broadcasted_iota(jnp.int32, (ITEM_ROWS, pair), 1) < head_dim

    def heads(hp, carry):
        head_gradients(
            lambda rows, cols: qkv_ref[rows, cols],
            lambda rows, cols: gmix_ref[rows, cols],
            lambda item, half: p_ref[item, hp * 2 + half],
            gqkv_ref, 0, hp, width, left,
        )
        return carry

    lax.fori_loop(0, HEADS // 2, heads, 0)
    unit, inverse = normalize_parts(x_ref[...].astype(F32))
    a = (unit * gain1_ref[...]).astype(BF16)
    for part in range(3):
        cols = slice(part * width, (part + 1) * width)
        gw = dot(a, gqkv_ref[:, cols], 0, 0)
        if n_carry:
            gw = gw + carried[0][:, cols]
        gwqkv_ref[:, cols] = gw
    gnorm = dot(gqkv_ref[...], wqkv_ref[...], 1, 1)
    gain1_grad = jnp.sum(gnorm * unit, axis=0, keepdims=True)
    gains = jnp.concatenate([gain1_grad, gain2_grad, jnp.zeros((6, width), F32)], axis=0)
    if n_carry:
        gains = gains + carried[2][...]
    ggain_ref[...] = gains
    tg_ref[...] = (gy + normalize_back(gnorm * gain1_ref[...], unit, inverse)).astype(BF16)


def attention_backward(parts, cot, x, y, qkv, p, o, gain1, gain2, wqkv, wo, carried):
    rows, width = x.shape
    out = jax.ShapeDtypeStruct
    return pl.pallas_call(
        functools.partial(attention_backward_kernel, len(parts), len(carried)),
        out_shape=(
            out((rows, width), BF16),
            out((width, 3 * width), F32),
            out((width, width), F32),
            out((8, width), F32),
        ),
        scratch_shapes=[pltpu.VMEM((rows, width), BF16), pltpu.VMEM((rows, 3 * width), BF16)],
        compiler_params=pltpu.CompilerParams(vmem_limit_bytes=VMEM_LIMIT),
        cost_estimate=pl.CostEstimate(
            flops=2 * rows * width * width * 8 + 16 * HEADS * ITEMS * ITEM_ROWS**2 * 128,
            bytes_accessed=30_000_000,
            transcendentals=0,
        ),
        name="attention_backward",
    )(*parts, cot, x, y, qkv, p, o, gain1, gain2, wqkv, wo, *carried)


def expert_kernel(groups, batches, pieces, *refs):
    flags, own_ref, more_ref, b_in, g_in, z_out, gb_out, gw_out = refs[:8]
    rows_b, rows_g, w, grads, in_sem, w_sem, out_sem, gw_sem = refs[8:]
    part = own_ref.shape[2]

    def rounded(rows):
        return (rows + TILE - 1) // TILE * TILE

    merged = [
        flags[g, 0, micro * ITEMS + item]
        for g in range(groups)
        for micro in range(batches)
        for item in range(ITEMS)
    ]
    n_merged = sum(merged)
    n_plain = len(merged) - n_merged
    sizes = [n_plain * IMAGE_ROWS, n_plain * CAPTION, n_merged * ITEM_ROWS]
    starts = [0, rounded(sizes[0]), rounded(sizes[0]) + rounded(sizes[1])]
    ends = [start + rounded(size) for start, size in zip(starts, sizes)]
    blocks = []
    plain, joined = 0, 0
    for flat, flag in enumerate(merged):
        g, micro, item = flat // (batches * ITEMS), flat // ITEMS % batches, flat % ITEMS
        base = item * ITEM_ROWS
        image = jnp.where(flag == 1, starts[2] + joined * ITEM_ROWS, plain * IMAGE_ROWS)
        caption = jnp.where(
            flag == 1, image + IMAGE_ROWS, starts[1] + plain * CAPTION
        )
        blocks.append((g, micro, base, IMAGE_ROWS, image, flag, 0))
        blocks.append((g, micro, base + IMAGE_ROWS, CAPTION, caption, flag, 1))
        plain, joined = plain + 1 - flag, joined + flag

    def copy_of(which, number, outward):
        g, micro, base, size, at, _, _ = blocks[number]
        held = (rows_b, rows_g)[which].at[pl.ds(pl.multiple_of(at, 16), size)]
        if outward:
            far = (gb_out, z_out)[which].at[g, micro, pl.ds(base, size)]
            return pltpu.make_async_copy(held, far, out_sem.at[which, number])
        far = (b_in, g_in)[which].at[g, micro, pl.ds(base, size)]
        return pltpu.make_async_copy(far, held, in_sem.at[which, number])

    def of_expert(expert, act):
        for number, (_, _, _, _, _, flag, kind) in enumerate(blocks):
            if expert == 2 or kind == expert:
                @pl.when(flag == (1 if expert == 2 else 0))
                def _(number=number):
                    for which in range(2):
                        act(which, number)

    def weight_copy(k, i):
        piece = own_ref if i == 0 else more_ref.at[i - 1]
        return pltpu.make_async_copy(
            piece.at[k], w.at[k, :, pl.ds(i * part, part), :], w_sem.at[k, i]
        )

    for k in range(3):
        tail = pl.multiple_of(jnp.maximum(ends[k] - TILE, 0), TILE)
        rows_b[pl.ds(tail, TILE), :] = jnp.zeros((TILE, rows_b.shape[1]), BF16)
        rows_g[pl.ds(tail, TILE), :] = jnp.zeros((TILE, rows_g.shape[1]), BF16)
    for k in range(3):
        of_expert(k, lambda which, number: copy_of(which, number, False).start())
        for i in range(pieces):
            weight_copy(k, i).start()

    third = w.shape[2] // 3
    for k in range(3):
        grads[...] = jnp.zeros(grads.shape, F32)
        of_expert(k, lambda which, number: copy_of(which, number, False).wait())
        for i in range(pieces):
            weight_copy(k, i).wait()

        def tile(t, carry, k=k):
            at = pl.ds(pl.multiple_of(t * TILE, TILE), TILE)
            b, gz = rows_b[at, :], rows_g[at, :]
            z = gb = None
            for c in range(3):
                cols = slice(c * third, (c + 1) * third)
                w1, w2 = w[k, 0, cols], w[k, 1, cols]
                u, slope = gelu_and_slope(dot(b, w1, 1, 1))
                gh = (dot(gz, w2, 1, 1) * slope).astype(BF16)
                u = u.astype(BF16)
                more_z, more_gb = dot(u, w2, 1, 0), dot(gh, w1, 1, 0)
                z = more_z if c == 0 else z + more_z
                gb = more_gb if c == 0 else gb + more_gb
                grads[0, cols] += dot(gh, b, 0, 0)
                grads[1, cols] += dot(u, gz, 0, 0)
            rows_b[at, :] = gb.astype(BF16)
            rows_g[at, :] = z.astype(BF16)
            return carry

        lax.fori_loop(starts[k] // TILE, ends[k] // TILE, tile, 0)
        of_expert(k, lambda which, number: copy_of(which, number, True).start())
        w[k] = grads[...].astype(BF16)
        for i in range(pieces):
            pltpu.make_async_copy(
                w.at[k, :, pl.ds(i * part, part), :], gw_out.at[i, k], gw_sem.at[k, i]
            ).start()
    for number in range(len(blocks)):
        for which in range(2):
            copy_of(which, number, True).wait()
    for k in range(3):
        for i in range(pieces):
            pltpu.make_async_copy(
                w.at[k, :, pl.ds(i * part, part), :], gw_out.at[i, k], gw_sem.at[k, i]
            ).wait()


def experts(flags, own, more, b_groups, g_groups):
    groups, batches, rows, width = b_groups.shape
    part = own.shape[2]
    pieces = 1 + (more.shape[0] if more.ndim == 5 else 0)
    hidden = part * pieces
    count = groups * batches * ITEMS
    capacity = (count * ITEM_ROWS // TILE + 4) * TILE
    out = jax.ShapeDtypeStruct
    anywhere = pl.BlockSpec(memory_space=pl.ANY)
    return pl.pallas_call(
        functools.partial(expert_kernel, groups, batches, pieces),
        in_specs=[pl.BlockSpec(memory_space=pltpu.SMEM)] + [anywhere] * 4,
        out_specs=[anywhere] * 3,
        out_shape=[out(b_groups.shape, BF16)] * 2 + [out((pieces,) + own.shape, BF16)],
        scratch_shapes=[
            pltpu.VMEM((capacity, width), BF16),
            pltpu.VMEM((capacity, width), BF16),
            pltpu.VMEM((3, 2, hidden, width), BF16),
            pltpu.VMEM((2, hidden, width), F32),
            pltpu.SemaphoreType.DMA((2, 2 * count)),
            pltpu.SemaphoreType.DMA((3, pieces)),
            pltpu.SemaphoreType.DMA((2, 2 * count)),
            pltpu.SemaphoreType.DMA((3, pieces)),
        ],
        compiler_params=pltpu.CompilerParams(vmem_limit_bytes=VMEM_LIMIT),
        cost_estimate=pl.CostEstimate(
            flops=2 * 6 * count * ITEM_ROWS * width * hidden,
            bytes_accessed=45_000_000,
            transcendentals=count * ITEM_ROWS * hidden,
        ),
        name="experts",
    )(flags, own, more, b_groups, g_groups)


def rows_of_items(first):
    row = jnp.arange(ROWS, dtype=jnp.int32)
    item, inside = row // ITEM_ROWS, row % ITEM_ROWS
    caption = jnp.where(first, item, 1 - item)
    return jnp.where(
        inside < PATCHES,
        item * PATCHES + inside,
        jnp.where(
            inside < IMAGE_ROWS,
            -1,
            ITEMS * PATCHES + caption * CAPTION + inside - IMAGE_ROWS,
        ),
    )


def to_items(rows, first):
    images = ITEMS * PATCHES
    one, two = rows[images : images + CAPTION], rows[images + CAPTION :]
    gap = jnp.zeros((IMAGE_ROWS - PATCHES,) + rows.shape[1:], rows.dtype)
    return jnp.concatenate(
        [
            rows[:PATCHES],
            gap,
            jnp.where(first, one, two),
            rows[PATCHES:images],
            gap,
            jnp.where(first, two, one),
        ],
        axis=0,
    )


def from_items(rows, first):
    one, two = rows[IMAGE_ROWS:ITEM_ROWS], rows[ITEM_ROWS + IMAGE_ROWS :]
    return jnp.concatenate(
        [
            rows[:PATCHES],
            rows[ITEM_ROWS : ITEM_ROWS + PATCHES],
            jnp.where(first, one, two),
            jnp.where(first, two, one),
        ],
        axis=0,
    )


def kept_tokens(routing, priority, hosts, capacity):
    length = routing.shape[0]
    index = jnp.arange(length, dtype=jnp.int32)
    position = jnp.sum(
        jnp.where(priority[None, :] == index[:, None], index[None, :], 0), axis=1
    )
    ahead = (routing[None, :] == routing[:, None]) & (position[None, :] < position[:, None])
    rank = jnp.sum(ahead.astype(jnp.int32), axis=1)
    return rank < capacity * ((hosts - routing + 2) // 3)


class Links:
    def __init__(self):
        self.hosts = lax.axis_size("expert")
        self.dp = lax.axis_size("dp")
        self.direct = self.hosts == 4 and self.dp == 8
        self.me = lax.axis_index("expert")

    def flip(self, v, bit):
        return lax.ppermute(v, "expert", [(i, i ^ bit) for i in range(4)])

    def across_y(self, v):
        return lax.ppermute(v, "dp", [(i, i ^ 1) for i in range(8)])

    def along_z(self, v, shift):
        return lax.ppermute(v, "dp", [(i, (i + 2 * shift) % 8) for i in range(8)])

    def gather_tokens(self, v):
        if not self.direct:
            return list(lax.all_gather(v, "expert"))
        near, far = self.flip(v, 1), self.flip(v, 2)
        return [v, near, far, self.flip(far, 1)]

    def reduce_tokens(self, parts):
        if not self.direct:
            return [lax.psum_scatter(jnp.stack(parts), "expert", scatter_dimension=0)]
        far = (parts[2].astype(F32) + self.flip(parts[3], 1).astype(F32)).astype(BF16)
        return [parts[0], self.flip(parts[1], 1), self.flip(far, 2)]

    def reduce_weights(self, pieces):
        if not self.direct:
            return lax.psum_scatter(pieces[0], "dp", scatter_dimension=2, tiled=True)
        total = None
        for at, shift in enumerate((0, 1, 3, 2)):
            piece = pieces[2 * at].astype(F32) + self.across_y(pieces[2 * at + 1]).astype(F32)
            if shift:
                piece = self.along_z(piece.astype(BF16), -shift).astype(F32)
            total = piece if total is None else total + piece
        return total.astype(BF16)

    def join_hidden(self, v):
        if not self.direct:
            return lax.all_gather(v, "expert", axis=2, tiled=True)
        stacked = jnp.stack(self.gather_tokens(v))
        return jnp.concatenate(
            [
                lax.dynamic_index_in_dim(stacked, i ^ self.me, 0, keepdims=False)
                for i in range(4)
            ],
            axis=2,
        )


def shards(
    tokens,
    cotangent,
    item_group,
    routes,
    slot_order,
    attn_gain,
    ffn_gain,
    qkv_weight,
    out_weight,
    expert_in,
    expert_out,
):
    links = Links()
    hosts, me = links.hosts, links.me
    batches, length, width = tokens.shape
    capacity = 2 * length // hosts
    shard = expert_in.shape[2]
    part = shard // hosts
    gain1, gain2 = attn_gain[None, :], ffn_gain[None, :]

    own = jnp.stack(
        [
            jnp.swapaxes(lax.dynamic_slice_in_dim(expert_in, me * part, part, 2), 1, 2),
            lax.dynamic_slice_in_dim(expert_out, me * part, part, 1),
        ],
        axis=1,
    )
    first = item_group[:, ITEMS * PATCHES] == 0
    merged = (routes[:, 0 : ITEMS * PATCHES : PATCHES] == 2).astype(jnp.int32)
    flags = jnp.broadcast_to(
        jnp.pad(merged.reshape(1, -1), ((0, 0), (0, 128 - batches * ITEMS))), (8, 128)
    )
    kept = jnp.stack(
        [kept_tokens(routes[m], slot_order[m, 0], hosts, capacity) for m in range(batches)]
    )
    index = jnp.stack([rows_of_items(first[m]) for m in range(batches)])[:, :, None]
    w_all, gz_groups, flag_groups, b_groups, x_all, qkv_all, p_all, o_all, y_all = front(
        links.direct, own, tokens, cotangent, index, kept.astype(F32)[:, None, :], flags,
        gain1, gain2, qkv_weight, out_weight,
    )
    if not links.direct:
        own = lax.all_gather(own, "dp", axis=2, tiled=True)
        gz_groups, flag_groups, b_groups = [
            lax.all_gather(v[0], "expert") for v in (gz_groups, flag_groups, b_groups)
        ]
    z_parts, gb_parts, gw_pieces = experts(flag_groups, own, w_all, b_groups, gz_groups)
    if links.direct:
        result, token_grad, gall, wsum, gains, *_ = back(
            gb_parts, z_parts, gw_pieces, cotangent, index, kept.astype(F32)[:, None, :],
            x_all, o_all, y_all, qkv_all, p_all, gain1, gain2, qkv_weight, out_weight,
        )
        shape = (3, hosts * part, width)
        wsum = wsum.astype(F32)
        return (
            result,
            token_grad,
            gains[0],
            gains[1],
            gall[:, : 3 * width].astype(F32),
            gall[:, 3 * width :].astype(F32),
            jnp.transpose(wsum[:, :, 0], (1, 3, 0, 2)).reshape(3, width, hosts * part),
            jnp.transpose(wsum[:, :, 1], (1, 0, 2, 3)).reshape(shape),
        )
    cot_items = [to_items(cotangent[m], first[m]) for m in range(batches)]
    gb_terms = links.reduce_tokens(gb_parts)
    z_terms = links.reduce_tokens(z_parts)
    sums = links.join_hidden(links.reduce_weights(gw_pieces)).astype(F32)

    results, token_grads, carried = [], [], ()
    for m in range(batches):
        x, qkv, p, o, y = x_all[m], qkv_all[m], p_all[m], o_all[m], y_all[m]
        at = m
        tg, *carried = attention_backward(
            [t[at] for t in gb_terms],
            cot_items[m], x, y, qkv, p, o, gain1, gain2, qkv_weight, out_weight,
            tuple(carried),
        )
        token_grads.append(from_items(tg, first[m]))
        z = z_terms[0][at].astype(F32)
        for term in z_terms[1:]:
            z = z + term[at].astype(F32)
        branch = jnp.where(kept[m][:, None], from_items(z, first[m]), 0.0)
        results.append((from_items(y, first[m]) + branch).astype(BF16))
    gw_qkv, gw_out, gains = carried
    packed = jnp.concatenate(
        [
            jnp.concatenate([gw_qkv, gw_out], axis=1),
            jnp.pad(gains[:2].reshape(1, 2 * width), ((0, 7), (0, 2 * width))),
        ],
        axis=0,
    ).astype(BF16)
    packed = lax.psum(packed, ("dp", "expert")).astype(F32)
    return (
        jnp.stack(results),
        jnp.stack(token_grads),
        packed[width, :width],
        packed[width, width : 2 * width],
        packed[:width, : 3 * width],
        packed[:width, 3 * width :],
        jnp.swapaxes(sums[:, 0], 1, 2),
        sums[:, 1],
    )


def solution(mesh):
    in_specs = (
        P(None, ("dp", "expert"), None),
        P(None, ("dp", "expert"), None),
        P(None, ("dp", "expert")),
        P(None, ("dp", "expert")),
        P(None, ("dp", "expert"), None),
        P(),
        P(),
        P(),
        P(),
        P(None, None, "dp"),
        P(None, "dp", None),
    )
    out_specs = (
        P(None, ("dp", "expert"), None),
        P(None, ("dp", "expert"), None),
        P(),
        P(),
        P(),
        P(),
        P(None, None, "dp"),
        P(None, "dp", None),
    )
    return jax.shard_map(shards, mesh=mesh, in_specs=in_specs, out_specs=out_specs, check_vma=False)
```

time: 1020 us -> 388 us (0.38)
  waiting for transfers between devices: 363 us -> 0 us
  matrix products: 340 us -> 0 us
  Pallas kernels: 0 us -> 339 us
  local copies, waits for them, and re-layouts: 138 us -> 30.9 us
  other arithmetic: 71.2 us -> 11.8 us
  blocking collectives: 42.2 us -> 0 us
  starting transfers between devices: 41.5 us -> 0 us
  between operations: 15.9 us -> 0.98 us
    dot_general x44 -> x0, matrix products: 340 us -> none  [the longest x12 71.4 us: contract_rows(): lax.dot_general(former, latter, (((0,), (0,)), ((), ())), preferred_eleme...]
    pallas_call x0 -> x3, Pallas kernels: none -> 339 us  [the longest x1 186 us: back(): pl.pallas_call(functools.partial(back_kernel, batches), in_specs=[anywher...]
    psum x2 -> x0, waiting for transfers between devices: 273 us -> none  [the longest x1 137 us: shards(): lax.psum((grad_qkv, grad_proj, grad_gain_one, grad_gain_two), ('dp', 'exp...]
    all_to_all x8 -> x0, waiting for transfers between devices: 72.3 us -> none  [the longest x2 23.4 us: shards(): lax.all_to_all(expert_rows, 'expert', split_axis=0, concat_axis=0, tiled=...]
    reshape x16 -> x1, local copies, waits for them, and re-layouts: 48.2 us -> 0.09 us  [shards(): merged.reshape(1, -1)]
    psum x1 -> x0, blocking collectives: 42.2 us -> none  [shards(): lax.psum((grad_qkv, grad_proj, grad_gain_one, grad_gain_two), ('dp', 'exp...]
    all_to_all x8 -> x0, starting transfers between devices: 40.9 us -> none  [the longest x2 10.6 us: shards(): lax.all_to_all(grad_back, 'expert', split_axis=0, concat_axis=0, tiled=True)]
    slice x13 -> x5, local copies, waits for them, and re-layouts: 29.8 us -> 4.23 us  [the longest x1 1.43 us: shards(): gains[1]]
  transfers between devices with their start and end apart: 14 -> 0, of which waited for: 10 -> 0; matrix products, arithmetic and copies ran while one was open for 52% -> 0% of each run, Pallas kernels for 0% -> 0%
where the time goes in v1:
time: 388 us; the launch traced here: 382 us
  Pallas kernels  339 us (87%)
  local copies, waits for them, and re-layouts  30.9 us (8%)
  other arithmetic  11.8 us (3%)
    pallas_call x1, Pallas kernels, back(): pl.pallas_call(functools.partial(back_kernel, batches), in_specs=[anywher...  186 us
    pallas_call x1, Pallas kernels, front(): pl.pallas_call(functools.partial(front_kernel, direct, batches), in_specs...  85.8 us
    pallas_call x1, Pallas kernels, experts(): pl.pallas_call(functools.partial(expert_kernel, groups, batches, pieces),...  67.3 us
    unnamed x18, local copies, waits for them, and re-layouts  16.2 us

profile of v1, /device:TPU:9, one launch (start us, length us, event | category | flops | bytes accessed | tf_op | source)
XLA Modules:
  0.0 382.4 jit_solution(7005843815714806873)
XLA Ops:
  0.7 0.9 slice_compare_fusion
  1.5 0.5 fusion.3
  2.1 0.8 slice.51
  2.9 1.3 broadcast_in_dim.57.refs_6_.refs_11_
  4.2 1.3 broadcast_in_dim.58.refs_7_.refs_12_
  5.5 0.6 broadcast_in_dim.56.refs_5_
  6.1 1.3 compare_select_fusion.2
  7.4 0.7 slice_reduce_fusion.3
  8.1 0.4 select_reduce_fusion
  8.5 0.8 slice_reduce_fusion.5
  9.3 0.4 convert_reduce_fusion.1
  9.7 0.4 convert_reduce_fusion
  10.1 0.8 compare_bitcast_fusion.1
  11.0 0.6 add_convert_fusion.refs_4_.refs_5_
  11.6 1.0 copy.39.refs_3_.refs_4_
  12.7 1.5 constant_dynamic-slice_fusion
  14.4 1.0 pad_maximum_fusion.refs_0_.refs_1_
  15.4 2.9 copy.38.refs_2_.refs_3_
  18.3 1.4 copy.37.refs_1_
  19.7 85.8 %front.1 = (bf16[7,3,2,96,768]{4,3,2,1,0:T(8,128)(2,1)}, bf16[4,2,544,768]{3,2,1,0:T(8,128)(2,1)}, s32[4,8,128]{2,1,0:T(8,128)}, bf16[4,2,544,768]{3,2,1,0:T(8,1...) custom-call(bf16[3,2,96,768]{3,2,1,0:T(8,128)(2,1)} %pad_maximum_fus, ...), custom_call_target="tpu_custom_call" | custom-call | flops 8770289664 | bytes 60000000 | tf_op jit(solution)/shard_map/front/pallas_call | solution.py:231
  105.4 67.3 %experts.1 = (bf16[4,2,544,768]{3,2,1,0:T(8,128)(2,1)}, bf16[4,2,544,768]{3,2,1,0:T(8,128)(2,1)}, bf16[8,3,2,96,768]{4,3,2,1,0:T(8,128)(2,1)}) custom-call(s32[4,8,128]{2,1,0:T(8,128)} %get-tuple-element.25.refs_0_, bf16[3,2,96,768]{3,2,1,0:T(8,128)(2,1)} %pad_maximum_fusion.refs_0_.refs_1_, bf16[7,3,2,96,768]{4,3,2,1,0:T(8,128)(2,1)} %get-tuple-element.26.refs_2_, ...), custom_call_target="tpu_custom_call" | custom-call | flops 30802968576 | bytes 45000000 | tf_op jit(solution)/shard_map/experts/pallas_call | solution.py:865
  172.7 185.7 %back.1 = (bf16[2,522,768]{2,1,0:T(8,128)(2,1)}, bf16[2,522,768]{2,1,0:T(8,128)(2,1)}, bf16[768,3072]{1,0:T(8,128)(2,1)}, bf16[4,3,2,96,768]{4,3,2,1,0:T(8,128)(...) custom-call(bf16[4,2,544,768]{3,2,1,0:T(8,128)(2,1)} %get-tuple-elem, ...), custom_call_target="tpu_custom_call" | custom-call | flops 17540579328 | bytes 80000000 | tf_op jit(solution)/shard_map/back/pallas_call | solution.py:639
  358.5 4.0 %copy.44 = bf16[2,522,768]{2,0,1:T(2,128)(2,1)} copy(bf16[2,522,768]{2,1,0:T(8,128)(2,1)} %get-tuple-element.58) | data formatting | bytes 3207168
  362.4 1.4 slice_reduce_fusion
  363.8 2.4 copy.45
  366.2 1.6 slice_convert_fusion.1
  367.8 3.5 slice_convert_fusion
  371.4 0.8 convert_element_type.32
  372.2 0.7 slice_bitcast_fusion
  372.9 2.0 copy.43
  374.9 2.0 copy.42
  376.9 5.3 %copy.46 = f32[3,768,384]{2,1,0:T(8,128)} copy(f32[3,768,384]{1,2,0:T(8,128)} %bitcast.27) | data formatting | bytes 7077888
  (18 shorter events, 0.4 us)
Async XLA Ops:
  0.6 10.9 %copy-start = (bf16[3,384,768]{2,1,0:T(8,128)(2,1)S(1)}, bf16[3,384,768]{2,1,0:T(8,128)(2,1)}, u32[]{:S(2)}) copy-start(bf16[3,384,768]{2,1,0:T(8,128)(2,1)} %param.21) | copy-start | bytes 5308420
  15.4 2.9 copy-start.5
  358.4 5.4 %copy-start.4 = (bf16[2,522,768]{2,1,0:T(8,128)(2,1)S(1)}, bf16[2,522,768]{2,1,0:T(8,128)(2,1)}, u32[]{:S(2)}) copy-start(bf16[2,522,768]{2,1,0:T(8,128)(2,1)} %get-tuple-element.59) | copy-start | bytes 4810756
  358.4 7.8 %copy-start.2 = (bf16[768,3072]{1,0:T(8,128)(2,1)S(1)}, bf16[768,3072]{1,0:T(8,128)(2,1)}, u32[]{:S(2)}) copy-start(bf16[768,3072]{1,0:T(8,128)(2,1)} %get-tuple-element.40) | copy-start | bytes 14155780
  367.8 3.5 copy-start.3
  376.9 5.3 %copy-start.1 = (bf16[3,384,768]{2,1,0:T(8,128)(2,1)S(1)}, bf16[3,384,768]{2,1,0:T(8,128)(2,1)}, u32[]{:S(2)}) copy-start(bf16[3,384,768]{2,1,0:T(8,128)(2,1)} %param.21) | copy-start | bytes 5308420
